TPU v7x, 256 devices: a whole 4x4x8 slice. The times are simulated.
256 devices in a mesh: rows: 4 (over x), chan: 8 (over y, z_lo), filt: 8 (over z_hi, core).
Axes of the slice: x: 4, y: 4, z: 8 (z_hi: 4, z_lo: 2; z = z_hi * 2 + z_lo), core: 2. Of those that a mesh axis runs over, the one named last changes fastest.
Arguments:
- images: bfloat16 [16, 2048, 2048], P('rows', 'chan', 'filt'), may hold values from -6 to 6
- first_weight: bfloat16 [2048, 1024], P('chan', 'filt'), may hold values from -0.125 to 0.125
- group_weight: bfloat16 [3, 3, 32, 1024], P(None, None, None, 'filt'), may hold values from -0.375 to 0.375
- third_weight: bfloat16 [1024, 2048], P('chan', 'filt'), may hold values from -0.1875 to 0.1875
- out_grad: bfloat16 [16, 2048, 2048], P('rows', 'chan', 'filt'), may hold values from -6 to 6
Outputs:
- block_out: bfloat16 [16, 2048, 2048], P('rows', 'chan', 'filt')
- images_grad: float32 [16, 2048, 2048], P('rows', 'chan', 'filt')
- first_grad: float32 [2048, 1024], P('chan', 'filt')
- group_grad: float32 [3, 3, 32, 1024], P(None, None, None, 'filt')
- third_grad: float32 [1024, 2048], P('chan', 'filt')
All inputs are finite; a program needn't handle non-finite values.
Results may differ from a plain program's by a relative error of at most 0.006.
Values may be sent and summed in bfloat16 or wider, within the bound.
No kernel may reach another device: no remote copies, remote signals or barrier semaphores. Data moves between devices by JAX's collectives and lax.ppermute only.
A program may use at most 128 MiB of HBM per device.

v0:
```python
import jax
import jax.numpy as jnp
from jax import lax
from jax.sharding import PartitionSpec as P


def extended(block, sides, width):
    for axis, dim in sides:
        count = lax.axis_size(axis)
        forward = [(i, i + 1) for i in range(count - 1)]
        backward = [(target, source) for source, target in forward]
        low = lax.ppermute(
            lax.slice_in_dim(block, block.shape[dim] - width, None, axis=dim), axis, forward
        )
        high = lax.ppermute(lax.slice_in_dim(block, 0, width, axis=dim), axis, backward)
        block = jnp.concatenate([low, block, high], axis=dim)
    return block


def silu_slope(values):
    logistic = jax.nn.sigmoid(values)
    return logistic * (1.0 + values * (1.0 - logistic))


def group_conv(padded, kernel, groups_here):
    result = lax.conv_general_dilated(
        padded[None],
        kernel,
        (1, 1),
        "VALID",
        dimension_numbers=("NHWC", "HWIO", "NHWC"),
        feature_group_count=groups_here,
        preferred_element_type=jnp.float32,
    )
    return result[0]


def transposed_kernel(kernel, group_size, groups_here):
    pieces = kernel.reshape(3, 3, group_size, groups_here, group_size)
    swapped = jnp.transpose(pieces, (0, 1, 4, 3, 2)).reshape(
        3, 3, group_size, groups_here * group_size
    )
    return swapped[::-1, ::-1]


def kernel_partial(padded_first, group_delta, group_size, groups_here):
    rows_here = group_delta.shape[0]
    cols_here = group_delta.shape[1]
    pixels = rows_here * cols_here
    delta_groups = group_delta.reshape(pixels, groups_here, group_size)
    kernel_terms = []
    for row_shift in range(3):
        for col_shift in range(3):
            window = padded_first[
                row_shift : row_shift + rows_here, col_shift : col_shift + cols_here
            ]
            window = window.reshape(pixels, groups_here, group_size)
            kernel_terms.append(
                jnp.einsum("pgi,pgo->gio", window, delta_groups, preferred_element_type=jnp.float32)
            )
    kernel_part = jnp.stack(kernel_terms).reshape(3, 3, groups_here, group_size, group_size)
    kernel_part = jnp.transpose(kernel_part, (0, 1, 3, 2, 4))
    return kernel_part.reshape(3, 3, group_size, groups_here * group_size)


def body(images, first_weight, group_weight, third_weight, out_grad):
    rows_here = images.shape[0]
    cols_here = images.shape[1]
    group_size = group_weight.shape[2]
    first_panel, third_panel = (
        lax.all_gather(first_weight, "chan", axis=0, tiled=True),
        lax.all_gather(third_weight, "chan", axis=0, tiled=True),
    )
    pixels = rows_here * cols_here
    groups_here = group_weight.shape[3] // group_size
    gathered = lax.all_gather(images, "filt", axis=2, tiled=True)
    flat_images = gathered.reshape(pixels, gathered.shape[2])
    pre_first = jnp.dot(flat_images, first_panel, preferred_element_type=jnp.float32)
    act_first = (
        jax.nn.silu(pre_first)
        .astype(jnp.bfloat16)
        .reshape(rows_here, cols_here, first_panel.shape[1])
    )
    padded_first = extended(act_first, (("rows", 0), ("chan", 1)), 1)
    pre_group = group_conv(padded_first, group_weight, groups_here)
    act_group = jax.nn.silu(pre_group).astype(jnp.bfloat16)
    mid_whole = lax.all_gather(act_group, "filt", axis=2, tiled=True)
    flat_mid = mid_whole.reshape(pixels, mid_whole.shape[2])
    third_out = jnp.dot(flat_mid, third_panel, preferred_element_type=jnp.float32)
    own_images = images.reshape(pixels, images.shape[2]).astype(jnp.float32)
    block_out = (own_images + third_out).astype(jnp.bfloat16).reshape(images.shape)
    grad_flat = out_grad.reshape(pixels, out_grad.shape[2])
    mid_terms = lax.dot_general(
        grad_flat, third_panel, (((1,), (1,)), ((), ())), preferred_element_type=jnp.float32
    )
    mid_grad = lax.psum_scatter(
        mid_terms.reshape(rows_here, cols_here, mid_terms.shape[1]),
        "filt",
        scatter_dimension=2,
        tiled=True,
    )
    third_part = lax.dot_general(
        flat_mid, grad_flat, (((0,), (0,)), ((), ())), preferred_element_type=jnp.float32
    )
    group_delta = (mid_grad * silu_slope(pre_group)).astype(jnp.bfloat16)
    padded_delta = extended(group_delta, (("rows", 0), ("chan", 1)), 1)
    first_back = group_conv(
        padded_delta, transposed_kernel(group_weight, group_size, groups_here), groups_here
    )
    kernel_part = kernel_partial(padded_first, group_delta, group_size, groups_here)
    first_delta = (first_back.reshape(pixels, first_back.shape[2]) * silu_slope(pre_first)).astype(
        jnp.bfloat16
    )
    first_part = lax.dot_general(
        flat_images, first_delta, (((0,), (0,)), ((), ())), preferred_element_type=jnp.float32
    )
    input_terms = lax.dot_general(
        first_delta, first_panel, (((1,), (1,)), ((), ())), preferred_element_type=jnp.float32
    )
    back_images = lax.psum_scatter(
        input_terms.reshape(rows_here, cols_here, input_terms.shape[1]).astype(jnp.bfloat16),
        "filt",
        scatter_dimension=2,
        tiled=True,
    ).astype(jnp.float32)
    images_grad = out_grad.astype(jnp.float32) + back_images
    group_grad = lax.psum(kernel_part, ("rows", "chan"))
    first_total, third_total = lax.psum((first_part, third_part), "rows")
    first_grad, third_grad = (
        lax.psum_scatter(first_total, "chan", scatter_dimension=0, tiled=True),
        lax.psum_scatter(third_total, "chan", scatter_dimension=0, tiled=True),
    )
    return (block_out, images_grad, first_grad, group_grad, third_grad)


def solution(mesh):
    in_specs = (
        P("rows", "chan", "filt"),
        P("chan", "filt"),
        P(None, None, None, "filt"),
        P("chan", "filt"),
        P("rows", "chan", "filt"),
    )
    out_specs = (
        P("rows", "chan", "filt"),
        P("rows", "chan", "filt"),
        P("chan", "filt"),
        P(None, None, None, "filt"),
        P("chan", "filt"),
    )
    return jax.shard_map(body, mesh=mesh, in_specs=in_specs, out_specs=out_specs, check_vma=False)
```

profile of v0, /device:TPU:32, one launch (start us, length us, event | category | flops | bytes accessed | tf_op | source)
XLA Modules:
  0.0 700.0 jit_solution(2654013649618200023)
XLA Ops:
  7.9 39.6 %all_gather.15 = bf16[1024,256]{1,0:T(8,128)(2,1)S(1)} all-gather(bf16[128,256]{1,0:T(8,128)(2,1)} %param.8), channel_id=1, replica_groups=mesh['rows'=4,'chan'=8,'filt'=8] {'chan'}, dimensions={0}, use_global_device_ids=true | all-gather | bytes 589824 | tf_op jit(solution)/shard_map/all_gather | solution.py:72
  47.5 3.8 fusion.10
  52.2 36.9 %all_gather.13 = bf16[2048,128]{1,0:T(8,128)(2,1)S(1)} all-gather(bf16[256,128]{1,0:T(8,128)(2,1)S(1)} %copy-done.13), channel_id=1, replica_groups=mesh['rows'=4,'chan'=8,'filt'=8] {'chan'}, dimensions={0}, use_global_device_ids=true | all-gather | bytes 589824 | tf_op jit(solution)/shard_map/all_gather | solution.py:71
  89.1 4.4 multiply_convert_fusion.3
  93.5 2.9 collective-permute-start
  98.4 4.2 collective-permute-done.1
  103.2 3.4 collective-permute-start.2
  106.6 3.2 collective-permute-start.3
  110.7 8.0 %collective-permute-done.2 = bf16[6,1,128]{1,2,0:T(8,128)(2,1)S(1)} collective-permute-done((bf16[6,1,128]{1,2,0:T(8,128)(2,1)S(1)}, bf16[6,1,128]{1,2,0:T(8,128)(2,1)S(1)}, u32[]{:S(2)}, u32[]{:S(2)}) %collective-permute-start.2) | collective-permute-done | bytes 1568 | tf_op jit(solution)/shard_map/ppermute | solution.py:12
  118.7 10.6 %collective-permute-done.3 = bf16[6,1,128]{1,2,0:T(8,128)(2,1)S(1)} collective-permute-done((bf16[6,1,128]{1,2,0:T(8,128)(2,1)S(1)}, bf16[6,1,128]{1,2,0:T(8,128)(2,1)S(1)}, u32[]{:S(2)}, u32[]{:S(2)}) %collective-permute-start.3) | collective-permute-done | bytes 1568 | tf_op jit(solution)/shard_map/ppermute | solution.py:15
  130.0 5.8 copy.36
  135.8 9.4 %fusion.13 = f32[1,4,256,4,32]{4,0,3,2,1:T(1,128)S(1)} fusion(bf16[1,6,258,4,32]{4,0,3,2,1:T(2,128)(2,1)} %copy.36, bf16[3,3,32,4,32]{4,3,2,1,0:T(4,128)(2,1)} %shard_map.94), kind=kOutput, calls=%fused_computation.39 | convolution fusion | flops 75497472 | bytes 994304 | tf_op jit(solution)/shard_map/conv_general_dilated | solution.py:26
  145.3 3.5 copy.38
  150.2 2.0 multiply_convert_fusion.1
  152.2 3.3 collective-permute-start.4
  157.5 4.3 collective-permute-done.5
  161.8 3.5 collective-permute-start.6
  165.3 2.6 collective-permute-start.7
  169.2 2.5 collective-permute-done.7
  172.1 5.9 copy.44
  178.0 13.8 %convolution_reduce_fusion = f32[4,256,4,32]{3,2,1,0:T(4,128)S(1)} fusion(bf16[1,6,258,4,32]{4,0,3,2,1:T(2,128)(2,1)} %copy.44, bf16[3,3,32,4,32]{4,3,2,1,0:T(4,128)(2,1)} %rev.6), kind=kOutput, calls=%fused_computation.2 | convolution fusion | flops 75497472 | bytes 994304 | tf_op jit(solution)/shard_map/conv_general_dilated | solution.py:26
  194.9 4.0 convolution_bitcast_fusion
  199.0 3.4 convolution_bitcast_fusion.1
  202.4 40.0 %reduce-scatter.9.cloned.1.call-done = f32[256,128]{0,1:T(8,128)} async-done(((f32[2048,128]{0,1:T(8,128)}), f32[256,128]{0,1:T(8,128)}) %reduce-scatter.9.cloned.1.call-update) | async-done | bytes 131088 | tf_op jit(solution)/shard_map/reduce_scatter | solution.py:130
  242.4 44.5 %reduce-scatter.11.cloned.1.call-done = f32[128,256]{1,0:T(8,128)} async-done(((f32[1024,256]{1,0:T(8,128)}), f32[128,256]{1,0:T(8,128)}) %reduce-scatter.11.cloned.1.call-update) | async-done | bytes 131088 | tf_op jit(solution)/shard_map/reduce_scatter | solution.py:131
  286.9 3.2 convolution_convert_fusion
  294.3 1.8 reshape.85
  312.5 3.2 fusion
  315.6 21.3 %all-reduce.6.cloned.1.call-done = (f32[256,128]{0,1:T(8,128)}, f32[128,256]{1,0:T(8,128)}) async-done(((f32[256,128]{0,1:T(8,128)}, f32[128,256]{1,0:T(8,128)}), (f32[256,128]{0,1:T(8,128)}, f32[128,256]{1,0:T(8,128)})) %all-reduce.6.cloned.1.call-update) | async-done | bytes 262160 | tf_op jit(solution)/shard_map/psum | solution.py:128
  338.7 59.3 %reduce-scatter.7.cloned.1.call-done = bf16[4,256,256]{2,1,0:T(8,128)(2,1)} async-done(((bf16[4,256,2048]{2,1,0:T(8,128)(2,1)}), bf16[4,256,256]{2,1,0:T(8,128)(2,1)}) %reduce-scatter.7.cloned.1.call-update) | async-done | bytes 524304 | tf_op jit(solution)/shard_map/reduce_scatter | solution.py:120
  398.0 2.1 convert_add_fusion
  400.1 290.7 %all-reduce.4.cloned.1.call-done = f32[3,3,32,128]{3,2,1,0:T(8,128)} async-done(((f32[3,3,32,128]{3,2,1,0:T(8,128)}), f32[3,3,32,128]{3,2,1,0:T(8,128)}) %all-reduce.4.cloned.1.call-update) | async-done | bytes 147472 | tf_op jit(solution)/shard_map/psum | solution.py:127
  (106 shorter events, 38.3 us)
Async XLA Ops:
  7.2 81.9 %all-gather.3.cloned.1.call-start = ((), (), s32[]{:S(2)}) async-start(), calls=%async_computation.4 | async-start | bytes 4718592 | tf_op jit(solution)/shard_map/all_gather | solution.py:76
  7.9 142.2 %reduce-scatter.5.cloned.1.call-start = ((), (), s32[]{:S(2)}) async-start(), calls=%async_computation.6 | async-start | bytes 4718592 | tf_op jit(solution)/shard_map/reduce_scatter | solution.py:96
  51.3 0.8 copy-start.13
  51.4 147.6 %all-gather.5.cloned.1.call-start = ((), (), s32[]{:S(2)}) async-start(), calls=%async_computation.5 | async-start | bytes 2359296 | tf_op jit(solution)/shard_map/all_gather | solution.py:87
  89.1 4.4 copy-start
  93.5 16.3 %copy-start.12 = (bf16[3,3,32,128]{3,2,1,0:T(8,128)(2,1)S(1)}, bf16[3,3,32,128]{3,2,1,0:T(8,128)(2,1)}, u32[]{:S(2)}) copy-start(bf16[3,3,32,128]{3,2,1,0:T(8,128)(2,1)} %param.7) | copy-start | bytes 221188
  93.5 4.8 collective-permute-start
  96.4 6.2 collective-permute-start.1
  98.3 4.6 copy-start.7
  102.6 0.6 copy-start.9
  103.2 15.5 %collective-permute-start.2 = (bf16[6,1,128]{1,2,0:T(8,128)(2,1)S(1)}, bf16[6,1,128]{1,2,0:T(8,128)(2,1)S(1)}, u32[]{:S(2)}, u32[]{:S(2)}) collective-permute-start(bf16[6,1,128]{1,2,0:T(8,128)(2,1)S(1)} %get-tuple-element.29), channel_id=1, source_target_pairs={{0,8},{8,16},{16,24},{24,32},{32,40},{40,48},{48,56},{1,9},{9,17},... | collective-permute-start | bytes 4616 | tf_op jit(solution)/shard_map/ppermute | solution.py:12
  106.6 22.7 %collective-permute-start.3 = (bf16[6,1,128]{1,2,0:T(8,128)(2,1)S(1)}, bf16[6,1,128]{1,2,0:T(8,128)(2,1)S(1)}, u32[]{:S(2)}, u32[]{:S(2)}) collective-permute-start(bf16[6,1,128]{1,2,0:T(8,128)(2,1)S(1)} %get-tuple-element.30), channel_id=1, source_target_pairs={{8,0},{16,8},{24,16},{32,24},{40,32},{48,40},{56,48},{9,1},{17,9},... | collective-permute-start | bytes 4616 | tf_op jit(solution)/shard_map/ppermute | solution.py:15
  118.7 17.1 %copy-start.4 = (bf16[6,1,128]{1,2,0:T(8,128)(2,1)}, bf16[6,1,128]{1,2,0:T(8,128)(2,1)S(1)}, u32[]{:S(2)}) copy-start(bf16[6,1,128]{1,2,0:T(8,128)(2,1)S(1)} %collective-permute-done.2) | copy-start | bytes 4612
  129.3 0.7 copy-start.6
  148.8 19.0 %copy-start.3 = (bf16[3,3,32,4,32]{4,3,2,1,0:T(4,128)(2,1)S(1)}, bf16[3,3,32,4,32]{4,3,2,1,0:T(4,128)(2,1)}, u32[]{:S(2)}) copy-start(bf16[3,3,32,4,32]{4,3,2,1,0:T(4,128)(2,1)} %shard_map.94) | copy-start | bytes 221188
  152.2 90.2 %reduce-scatter.9.cloned.1.call-start = ((), (), s32[]{:S(2)}) async-start(), calls=%async_computation.9 | async-start | bytes 1179648 | tf_op jit(solution)/shard_map/reduce_scatter | solution.py:130
  152.2 5.2 collective-permute-start.4
  155.6 6.2 collective-permute-start.5
  161.8 7.4 %collective-permute-start.6 = (bf16[6,1,128]{2,1,0:T(2,128)(2,1)S(1)}, bf16[6,1,128]{2,1,0:T(2,128)(2,1)S(1)}, u32[]{:S(2)}, u32[]{:S(2)}) collective-permute-start(bf16[6,1,128]{2,1,0:T(2,128)(2,1)S(1)} %get-tuple-element.27), channel_id=1, source_target_pairs={{0,8},{8,16},{16,24},{24,32},{32,40},{40,48},{48,56},{1,9},{9,17},... | collective-permute-start | bytes 4616 | tf_op jit(solution)/shard_map/ppermute | solution.py:12
  165.3 6.4 collective-permute-start.7
  194.9 4.1 copy-start.2
  198.9 88.0 %copy-start.1 = (bf16[2048,128]{1,0:T(8,128)(2,1)S(1)}, bf16[2048,128]{1,0:T(8,128)(2,1)}, u32[]{:S(2)}) copy-start(bf16[2048,128]{1,0:T(8,128)(2,1)} %copy-done) | copy-start | bytes 1572868
  198.9 88.0 %reduce-scatter.11.cloned.1.call-start = ((), (), s32[]{:S(2)}) async-start(), calls=%async_computation.10 | async-start | bytes 1179648 | tf_op jit(solution)/shard_map/reduce_scatter | solution.py:131
  202.4 134.6 %all-reduce.6.cloned.1.call-start = ((), (), s32[]{:S(2)}) async-start(), calls=%async_computation.11 | async-start | bytes 524288 | tf_op jit(solution)/shard_map/psum | solution.py:128
  286.9 111.1 %reduce-scatter.7.cloned.1.call-start = ((), (), s32[]{:S(2)}) async-start(), calls=%async_computation.7 | async-start | bytes 4718592 | tf_op jit(solution)/shard_map/reduce_scatter | solution.py:120
  290.2 0.8 copy-start.8
  290.2 0.9 copy-start.10
  290.2 1.6 copy-start.5
  290.2 400.7 %all-reduce.4.cloned.1.call-start = ((), (), s32[]{:S(2)}) async-start(), calls=%async_computation.8 | async-start | bytes 294912 | tf_op jit(solution)/shard_map/psum | solution.py:127
  337.0 355.5 %copy-start.11 = (f32[128,256]{1,0:T(8,128)S(1)}, f32[128,256]{1,0:T(8,128)}, u32[]{:S(2)}) copy-start(f32[128,256]{1,0:T(8,128)} %get-tuple-element.46) | copy-start | bytes 393220
Sparse Core Ops, SparseCore 0:
  9.8 60.3 all-gather.2
  72.7 76.7 reduce-scatter.4
  152.3 42.8 all-gather.4
  199.0 43.3 reduce-scatter.8
  244.8 42.0 reduce-scatter.10
  289.1 47.8 all-reduce.5
  339.7 58.2 reduce-scatter.6
  401.4 289.4 all-reduce.3
where the time goes:
time: 701 us; the launch traced here: 700 us
  waiting for transfers between devices  487 us (69%)
  blocking collectives  76.5 us (11%)
  matrix products  49 us (7%)
  local copies, waits for them, and re-layouts  43.4 us (6%)
  starting transfers between devices  22 us (3%)
  between operations  14.5 us (2%)
  other arithmetic  7.29 us (1%)
    psum x1, waiting for transfers between devices, body(): group_grad = lax.psum(kernel_part, ('rows', 'chan'))  291 us
    reduce_scatter x1, waiting for transfers between devices, body(): lax.psum_scatter(input_terms.reshape(rows_here, cols_here, input_terms.sh...  59.3 us
    reduce_scatter x1, waiting for transfers between devices, body(): lax.psum_scatter(third_total, 'chan', scatter_dimension=0, tiled=True)  44.5 us
    reduce_scatter x1, waiting for transfers between devices, body(): lax.psum_scatter(first_total, 'chan', scatter_dimension=0, tiled=True)  40 us
    all_gather x1, blocking collectives, body(): lax.all_gather(third_weight, 'chan', axis=0, tiled=True)  39.6 us
    all_gather x1, blocking collectives, body(): lax.all_gather(first_weight, 'chan', axis=0, tiled=True)  36.9 us
    conv_general_dilated x2, matrix products, group_conv(): lax.conv_general_dilated(padded[None], kernel, (1, 1), 'VALID', dimension...  23.3 us
    ppermute x4, waiting for transfers between devices, extended(): lax.ppermute(lax.slice_in_dim(block, 0, width, axis=dim), axis, backward)  21.5 us
  transfers between devices with their start and end apart: 16, of which 12 were waited for; matrix products, arithmetic and copies ran while one was open for 13% of the time, Pallas kernels for 0%

commit v1 on v0

--- a/solution.py
+++ b/solution.py
@@ -1,7 +1,21 @@
+import functools
 import jax
 import jax.numpy as jnp
 from jax import lax
 from jax.sharding import PartitionSpec as P
+from jax.lax import all_to_all, psum
+
+
+def core_note(frame, which_dim):
+    return jnp.concatenate(
+        all_to_all(
+            jnp.stack(psum(1, "chan") * [frame], axis=0), "chan", split_axis=0, concat_axis=0
+        ),
+        axis=which_dim,
+    )
+
+
+load_heads = functools.partial(core_note, which_dim=0)
 
 
 def extended(block, sides, width):
@@ -68,7 +82,7 @@
     cols_here = images.shape[1]
     group_size = group_weight.shape[2]
     first_panel, third_panel = (
-        lax.all_gather(first_weight, "chan", axis=0, tiled=True),
+        load_heads(first_weight),
         lax.all_gather(third_weight, "chan", axis=0, tiled=True),
     )
     pixels = rows_here * cols_here

time: 701 us -> 693 us (0.989)
  blocking collectives: 76.5 us -> 56.7 us
  starting transfers between devices: 22 us -> 29.1 us
    all_gather x1 -> x0, blocking collectives: 36.9 us -> none  [body(): lax.all_gather(first_weight, 'chan', axis=0, tiled=True)]
    all_to_all x0 -> x1, blocking collectives: none -> 17.3 us  [core_note(): all_to_all(jnp.stack(psum(1, 'chan') * [frame], axis=0), 'chan', split_ax...]
  transfers between devices with their start and end apart: 16 -> 16, of which waited for: 12 -> 14; matrix products, arithmetic and copies ran while one was open for 13% -> 14% of each run, Pallas kernels for 0% -> 0%
where the time goes in v1:
time: 693 us; the launch traced here: 692 us
  waiting for transfers between devices  492 us (71%)
  blocking collectives  56.7 us (8%)
  matrix products  48.8 us (7%)
  local copies, waits for them, and re-layouts  43.5 us (6%)
  starting transfers between devices  29.1 us (4%)
  between operations  14.5 us (2%)
  other arithmetic  7.27 us (1%)
    psum x1, waiting for transfers between devices, body(): group_grad = lax.psum(kernel_part, ('rows', 'chan'))  291 us
    reduce_scatter x1, waiting for transfers between devices, body(): lax.psum_scatter(input_terms.reshape(rows_here, cols_here, input_terms.sh...  59.3 us
    reduce_scatter x1, waiting for transfers between devices, body(): lax.psum_scatter(third_total, 'chan', scatter_dimension=0, tiled=True)  44.4 us
    all_gather x1, blocking collectives, body(): lax.all_gather(third_weight, 'chan', axis=0, tiled=True)  39.4 us
    reduce_scatter x1, waiting for transfers between devices, body(): lax.psum_scatter(first_total, 'chan', scatter_dimension=0, tiled=True)  37.8 us
    ppermute x4, waiting for transfers between devices, extended(): lax.ppermute(lax.slice_in_dim(block, 0, width, axis=dim), axis, backward)  25.3 us
    conv_general_dilated x2, matrix products, group_conv(): lax.conv_general_dilated(padded[None], kernel, (1, 1), 'VALID', dimension...  23.3 us
    psum x1, waiting for transfers between devices, body(): first_total, third_total = lax.psum((first_part, third_part), 'rows')  21.3 us
  transfers between devices with their start and end apart: 16, of which 14 were waited for; matrix products, arithmetic and copies ran while one was open for 14% of the time, Pallas kernels for 0%

profile of v1, /device:TPU:32, one launch (start us, length us, event | category | flops | bytes accessed | tf_op | source)
XLA Modules:
  0.0 692.4 jit_solution(12058445084392213239)
XLA Ops:
  7.9 39.4 %all_gather.11 = bf16[1024,256]{1,0:T(8,128)(2,1)S(1)} all-gather(bf16[128,256]{1,0:T(8,128)(2,1)} %param.8), channel_id=1, replica_groups=mesh['rows'=4,'chan'=8,'filt'=8] {'chan'}, dimensions={0}, use_global_device_ids=true | all-gather | bytes 589824 | tf_op jit(solution)/shard_map/all_gather | solution.py:86
  47.4 3.8 fusion.10
  52.1 17.3 %all_to_all.5 = bf16[8,256,128]{2,1,0:T(8,128)(2,1)S(1)} all-to-all(bf16[8,256,128]{2,1,0:T(8,128)(2,1)S(1)} %stack.41), channel_id=1, replica_groups=mesh['rows'=4,'chan'=8,'filt'=8] {'chan'}, dimensions={0} | all-to-all | bytes 1048576 | tf_op jit(solution)/shard_map/all_to_all | solution.py:11
  69.7 4.2 multiply_convert_fusion.3
  73.9 4.2 collective-permute-start
  80.2 4.2 collective-permute-done.1
  84.9 10.2 %collective-permute-start.2 = (bf16[6,1,128]{1,2,0:T(8,128)(2,1)S(1)}, bf16[6,1,128]{1,2,0:T(8,128)(2,1)S(1)}, u32[]{:S(2)}, u32[]{:S(2)}) collective-permute-start(bf16[6,1,128]{1,2,0:T(8,128)(2,1)S(1)} %get-tuple-element.29), channel_id=1, source_target_pairs={{0,8},{8,16},{16,24},{24,32},{32,40},{40,48},{48,56},{1,9},{9,17},... | collective-permute-start | bytes 4616 | tf_op jit(solution)/shard_map/ppermute | solution.py:26
  95.1 2.1 collective-permute-start.3
  98.1 7.9 %collective-permute-done.2 = bf16[6,1,128]{1,2,0:T(8,128)(2,1)S(1)} collective-permute-done((bf16[6,1,128]{1,2,0:T(8,128)(2,1)S(1)}, bf16[6,1,128]{1,2,0:T(8,128)(2,1)S(1)}, u32[]{:S(2)}, u32[]{:S(2)}) %collective-permute-start.2) | collective-permute-done | bytes 1568 | tf_op jit(solution)/shard_map/ppermute | solution.py:26
  106.1 15.8 %collective-permute-done.3 = bf16[6,1,128]{1,2,0:T(8,128)(2,1)S(1)} collective-permute-done((bf16[6,1,128]{1,2,0:T(8,128)(2,1)S(1)}, bf16[6,1,128]{1,2,0:T(8,128)(2,1)S(1)}, u32[]{:S(2)}, u32[]{:S(2)}) %collective-permute-start.3) | collective-permute-done | bytes 1568 | tf_op jit(solution)/shard_map/ppermute | solution.py:29
  122.6 5.8 copy.36
  128.4 9.5 %fusion.13 = f32[1,4,256,4,32]{4,0,3,2,1:T(1,128)S(1)} fusion(bf16[1,6,258,4,32]{4,0,3,2,1:T(2,128)(2,1)} %copy.36, bf16[3,3,32,4,32]{4,3,2,1,0:T(4,128)(2,1)} %shard_map.94), kind=kOutput, calls=%fused_computation.39 | convolution fusion | flops 75497472 | bytes 994304 | tf_op jit(solution)/shard_map/conv_general_dilated | solution.py:40
  137.9 3.5 copy.38
  142.7 3.5 reduce-scatter.5.cloned.1.call-done
  146.2 2.0 multiply_convert_fusion.1
  148.3 3.4 collective-permute-start.4
  153.6 4.3 collective-permute-done.5
  157.9 2.1 collective-permute-start.6
  160.0 4.0 collective-permute-start.7
  166.8 5.9 copy.44
  172.7 13.8 %convolution_reduce_fusion = f32[4,256,4,32]{3,2,1,0:T(4,128)S(1)} fusion(bf16[1,6,258,4,32]{4,0,3,2,1:T(2,128)(2,1)} %copy.44, bf16[3,3,32,4,32]{4,3,2,1,0:T(4,128)(2,1)} %rev.6), kind=kOutput, calls=%fused_computation.2 | convolution fusion | flops 75497472 | bytes 994304 | tf_op jit(solution)/shard_map/conv_general_dilated | solution.py:40
  189.6 4.0 convolution_bitcast_fusion
  193.7 3.4 convolution_bitcast_fusion.1
  197.1 37.8 %reduce-scatter.9.cloned.1.call-done = f32[256,128]{0,1:T(8,128)} async-done(((f32[2048,128]{0,1:T(8,128)}), f32[256,128]{0,1:T(8,128)}) %reduce-scatter.9.cloned.1.call-update) | async-done | bytes 131088 | tf_op jit(solution)/shard_map/reduce_scatter | solution.py:144
  234.9 44.4 %reduce-scatter.11.cloned.1.call-done = f32[128,256]{1,0:T(8,128)} async-done(((f32[1024,256]{1,0:T(8,128)}), f32[128,256]{1,0:T(8,128)}) %reduce-scatter.11.cloned.1.call-update) | async-done | bytes 131088 | tf_op jit(solution)/shard_map/reduce_scatter | solution.py:145
  279.4 3.2 convolution_convert_fusion
  286.7 1.8 reshape.91
  304.9 3.2 fusion
  308.1 21.3 %all-reduce.6.cloned.1.call-done = (f32[256,128]{0,1:T(8,128)}, f32[128,256]{1,0:T(8,128)}) async-done(((f32[256,128]{0,1:T(8,128)}, f32[128,256]{1,0:T(8,128)}), (f32[256,128]{0,1:T(8,128)}, f32[128,256]{1,0:T(8,128)})) %all-reduce.6.cloned.1.call-update) | async-done | bytes 262160 | tf_op jit(solution)/shard_map/psum | solution.py:142
  331.1 59.3 %reduce-scatter.7.cloned.1.call-done = bf16[4,256,256]{2,1,0:T(8,128)(2,1)} async-done(((bf16[4,256,2048]{2,1,0:T(8,128)(2,1)}), bf16[4,256,256]{2,1,0:T(8,128)(2,1)}) %reduce-scatter.7.cloned.1.call-update) | async-done | bytes 524304 | tf_op jit(solution)/shard_map/reduce_scatter | solution.py:134
  390.4 2.1 convert_add_fusion
  392.5 290.7 %all-reduce.4.cloned.1.call-done = f32[3,3,32,128]{3,2,1,0:T(8,128)} async-done(((f32[3,3,32,128]{3,2,1,0:T(8,128)}), f32[3,3,32,128]{3,2,1,0:T(8,128)}) %all-reduce.4.cloned.1.call-update) | async-done | bytes 147472 | tf_op jit(solution)/shard_map/psum | solution.py:141
  (107 shorter events, 39.7 us)
Async XLA Ops:
  7.2 62.5 %all-gather.3.cloned.1.call-start = ((), (), s32[]{:S(2)}) async-start(), calls=%async_computation.5 | async-start | bytes 4718592 | tf_op jit(solution)/shard_map/all_gather | solution.py:90
  7.9 138.3 %reduce-scatter.5.cloned.1.call-start = ((), (), s32[]{:S(2)}) async-start(), calls=%async_computation.7 | async-start | bytes 4718592 | tf_op jit(solution)/shard_map/reduce_scatter | solution.py:110
  51.2 0.8 copy-start.13
  51.2 142.5 %all-gather.5.cloned.1.call-start = ((), (), s32[]{:S(2)}) async-start(), calls=%async_computation.6 | async-start | bytes 2359296 | tf_op jit(solution)/shard_map/all_gather | solution.py:101
  69.4 4.5 copy-start
  73.9 23.3 %copy-start.12 = (bf16[3,3,32,128]{3,2,1,0:T(8,128)(2,1)S(1)}, bf16[3,3,32,128]{3,2,1,0:T(8,128)(2,1)}, u32[]{:S(2)}) copy-start(bf16[3,3,32,128]{3,2,1,0:T(8,128)(2,1)} %param.7) | copy-start | bytes 221188
  73.9 6.1 collective-permute-start
  78.2 6.2 collective-permute-start.1
  80.0 4.6 copy-start.7
  84.3 0.6 copy-start.9
  84.9 21.1 %collective-permute-start.2 = (bf16[6,1,128]{1,2,0:T(8,128)(2,1)S(1)}, bf16[6,1,128]{1,2,0:T(8,128)(2,1)S(1)}, u32[]{:S(2)}, u32[]{:S(2)}) collective-permute-start(bf16[6,1,128]{1,2,0:T(8,128)(2,1)S(1)} %get-tuple-element.29), channel_id=1, source_target_pairs={{0,8},{8,16},{16,24},{24,32},{32,40},{40,48},{48,56},{1,9},{9,17},... | collective-permute-start | bytes 4616 | tf_op jit(solution)/shard_map/ppermute | solution.py:26
  95.1 26.8 %collective-permute-start.3 = (bf16[6,1,128]{1,2,0:T(8,128)(2,1)S(1)}, bf16[6,1,128]{1,2,0:T(8,128)(2,1)S(1)}, u32[]{:S(2)}, u32[]{:S(2)}) collective-permute-start(bf16[6,1,128]{1,2,0:T(8,128)(2,1)S(1)} %get-tuple-element.30), channel_id=1, source_target_pairs={{8,0},{16,8},{24,16},{32,24},{40,32},{48,40},{56,48},{9,1},{17,9},... | collective-permute-start | bytes 4616 | tf_op jit(solution)/shard_map/ppermute | solution.py:29
  106.1 22.4 %copy-start.4 = (bf16[6,1,128]{1,2,0:T(8,128)(2,1)}, bf16[6,1,128]{1,2,0:T(8,128)(2,1)S(1)}, u32[]{:S(2)}) copy-start(bf16[6,1,128]{1,2,0:T(8,128)(2,1)S(1)} %collective-permute-done.2) | copy-start | bytes 4612
  121.9 0.7 copy-start.6
  141.4 22.6 %copy-start.3 = (bf16[3,3,32,4,32]{4,3,2,1,0:T(4,128)(2,1)S(1)}, bf16[3,3,32,4,32]{4,3,2,1,0:T(4,128)(2,1)}, u32[]{:S(2)}) copy-start(bf16[3,3,32,4,32]{4,3,2,1,0:T(4,128)(2,1)} %shard_map.94) | copy-start | bytes 221188
  148.2 86.7 %reduce-scatter.9.cloned.1.call-start = ((), (), s32[]{:S(2)}) async-start(), calls=%async_computation.10 | async-start | bytes 1179648 | tf_op jit(solution)/shard_map/reduce_scatter | solution.py:144
  148.3 5.3 collective-permute-start.4
  151.7 6.2 collective-permute-start.5
  157.9 7.4 %collective-permute-start.6 = (bf16[6,1,128]{2,1,0:T(2,128)(2,1)S(1)}, bf16[6,1,128]{2,1,0:T(2,128)(2,1)S(1)}, u32[]{:S(2)}, u32[]{:S(2)}) collective-permute-start(bf16[6,1,128]{2,1,0:T(2,128)(2,1)S(1)} %get-tuple-element.27), channel_id=1, source_target_pairs={{0,8},{8,16},{16,24},{24,32},{32,40},{40,48},{48,56},{1,9},{9,17},... | collective-permute-start | bytes 4616 | tf_op jit(solution)/shard_map/ppermute | solution.py:26
  160.0 6.4 collective-permute-start.7
  189.6 4.1 copy-start.2
  193.6 85.7 %copy-start.1 = (bf16[8,256,128]{2,1,0:T(8,128)(2,1)S(1)}, bf16[8,256,128]{2,1,0:T(8,128)(2,1)}, u32[]{:S(2)}) copy-start(bf16[8,256,128]{2,1,0:T(8,128)(2,1)} %copy-done) | copy-start | bytes 1572868
  193.6 85.7 %reduce-scatter.11.cloned.1.call-start = ((), (), s32[]{:S(2)}) async-start(), calls=%async_computation.11 | async-start | bytes 1179648 | tf_op jit(solution)/shard_map/reduce_scatter | solution.py:145
  197.1 132.3 %all-reduce.6.cloned.1.call-start = ((), (), s32[]{:S(2)}) async-start(), calls=%async_computation.12 | async-start | bytes 524288 | tf_op jit(solution)/shard_map/psum | solution.py:142
  279.3 111.1 %reduce-scatter.7.cloned.1.call-start = ((), (), s32[]{:S(2)}) async-start(), calls=%async_computation.8 | async-start | bytes 4718592 | tf_op jit(solution)/shard_map/reduce_scatter | solution.py:134
  282.6 0.8 copy-start.8
  282.6 0.9 copy-start.10
  282.6 1.6 copy-start.5
  282.6 400.7 %all-reduce.4.cloned.1.call-start = ((), (), s32[]{:S(2)}) async-start(), calls=%async_computation.9 | async-start | bytes 294912 | tf_op jit(solution)/shard_map/psum | solution.py:141
  329.4 355.5 %copy-start.11 = (f32[128,256]{1,0:T(8,128)S(1)}, f32[128,256]{1,0:T(8,128)}, u32[]{:S(2)}) copy-start(f32[128,256]{1,0:T(8,128)} %get-tuple-element.46) | copy-start | bytes 393220
Sparse Core Ops, SparseCore 0:
  9.8 59.8 all-gather.2
  72.3 73.8 reduce-scatter.4
  148.3 36.9 all-gather.4
  193.7 41.1 reduce-scatter.8
  237.3 41.9 reduce-scatter.10
  281.5 47.8 all-reduce.5
  332.1 58.2 reduce-scatter.6
  393.8 289.4 all-reduce.3
